TPU v7x, 128 devices: a whole 4x4x4 slice. The times are simulated.
128 devices in a mesh: worker: 16 (over x_lo, z, core), fsdp: 8 (over x_hi, y).
Axes of the slice: x: 4 (x_hi: 2, x_lo: 2; x = x_hi * 2 + x_lo), y: 4, z: 4, core: 2. Of those that a mesh axis runs over, the one named last changes fastest.
Arguments:
- tokens_x: bfloat16 [16384, 4096], P(('worker', 'fsdp')), may hold values from -24 to 24
- attn_out: bfloat16 [16384, 2048], P(('worker', 'fsdp')), may hold values from -24 to 24
- query_cot: bfloat16 [16384, 2048], P(('worker', 'fsdp')), may hold values from -0.5 to 0.5
- out_cot: bfloat16 [16384, 4096], P(('worker', 'fsdp')), may hold values from -0.5 to 0.5
- message_ids: int32 [16384], P(('worker', 'fsdp')), may hold values from 0 to 1023
- q_offset: float32 [16, 4096, 2048], P('worker', 'fsdp'), may hold values from -12 to 12
- q_first: bfloat16 [16, 4096, 2048], P('worker', 'fsdp'), may hold values from -1.5 to 1.5
- q_second: bfloat16 [16, 4096, 2048], P('worker', 'fsdp'), may hold values from 0.0009994507 to 0.099609375
- o_offset: float32 [16, 2048, 4096], P('worker', 'fsdp'), may hold values from -12 to 12
- o_first: bfloat16 [16, 2048, 4096], P('worker', 'fsdp'), may hold values from -1.5 to 1.5
- o_second: bfloat16 [16, 2048, 4096], P('worker', 'fsdp'), may hold values from 0.0009994507 to 0.099609375
- q_momentum: float32 [4096, 2048], P(('fsdp', 'worker')), may hold values from -6 to 6
- o_momentum: float32 [2048, 4096], P(('fsdp', 'worker')), may hold values from -6 to 6
Outputs:
- q_first_new: bfloat16 [16, 4096, 2048], P('worker', 'fsdp')
- o_first_new: bfloat16 [16, 2048, 4096], P('worker', 'fsdp')
- q_direction: float32 [4096, 2048], P(('fsdp', 'worker'))
- o_direction: float32 [2048, 4096], P(('fsdp', 'worker'))
- q_momentum_new: float32 [4096, 2048], P(('fsdp', 'worker'))
- o_momentum_new: float32 [2048, 4096], P(('fsdp', 'worker'))
All inputs are finite; a program needn't handle non-finite values.
Results may differ from a plain program's by a relative error of at most 0.019.
Values may be sent and summed in bfloat16 or wider, within the bound.
A program may use at most 192 MiB of HBM per device.

v0:
```python
import jax
import jax.numpy as jnp
from jax import lax
from jax.sharding import PartitionSpec as P

CONTROL = 256
STEP = 500
first_decay = 0.9
second_decay = 0.999
adam_eps = 1e-08
outer_mu = 0.9


def cross_rows(left, right):
    return lax.dot_general(
        left, right, (((0,), (0,)), ((), ())), preferred_element_type=jnp.float32
    )


def rounded(part):
    return lax.optimization_barrier(part.astype(jnp.bfloat16)).astype(jnp.float32)


def adam_moved(grads, offset, first, second):
    first_new = first_decay * first.astype(jnp.float32) + (1.0 - first_decay) * grads
    second_new = second_decay * second.astype(jnp.float32) + (1.0 - second_decay) * grads * grads
    first_hat = first_new / (1.0 - first_decay**STEP)
    second_hat = second_new / (1.0 - second_decay**STEP)
    moved = offset + first_hat / (jnp.sqrt(second_hat) + adam_eps)
    return (first_new.astype(jnp.bfloat16), moved)


def per_device(
    tokens_x,
    attn_out,
    query_cot,
    out_cot,
    message_ids,
    q_offset,
    q_first,
    q_second,
    o_offset,
    o_first,
    o_second,
    q_momentum,
    o_momentum,
):
    loss_mask = (message_ids >= CONTROL).astype(jnp.bfloat16)[:, None]
    q_cot = query_cot * loss_mask
    o_cot = out_cot * loss_mask
    tok_rows = tokens_x.shape[0]
    rows_q = q_offset.shape[1]
    rows_o = o_offset.shape[1]
    x_cols, a_cols = (
        lax.all_to_all(tokens_x, "fsdp", split_axis=1, concat_axis=0, tiled=True),
        lax.all_to_all(attn_out, "fsdp", split_axis=1, concat_axis=0, tiled=True),
    )
    first_row = jnp.int32(0)
    piece_q = lax.all_gather(q_cot, "fsdp", axis=0, tiled=True)
    piece_o = lax.all_gather(o_cot, "fsdp", axis=0, tiled=True)
    grads_q = jnp.zeros((rows_q, q_offset.shape[2]), jnp.float32)
    grads_o = jnp.zeros((rows_o, o_offset.shape[2]), jnp.float32)
    for number in range(piece_q.shape[0] // tok_rows):
        row = first_row + number * tok_rows
        left_q = lax.dynamic_slice_in_dim(x_cols, row, tok_rows, 0)
        left_o = lax.dynamic_slice_in_dim(a_cols, row, tok_rows, 0)
        right_q = piece_q[number * tok_rows : (number + 1) * tok_rows]
        right_o = piece_o[number * tok_rows : (number + 1) * tok_rows]
        grads_q = grads_q + rounded(cross_rows(left_q, right_q))
        grads_o = grads_o + rounded(cross_rows(left_o, right_o))
    q_first_new, moved_q = adam_moved(grads_q, q_offset[0], q_first[0], q_second[0])
    o_first_new, moved_o = adam_moved(grads_o, o_offset[0], o_first[0], o_second[0])
    workers = lax.axis_size("worker")
    total_q, total_o = (
        lax.psum(moved_q.astype(jnp.bfloat16), "worker").astype(jnp.float32),
        lax.psum(moved_o.astype(jnp.bfloat16), "worker").astype(jnp.float32),
    )
    worker_pos = lax.axis_index("worker")
    share_rows_q = rows_q // workers
    share_rows_o = rows_o // workers
    share_q = lax.dynamic_slice_in_dim(total_q, worker_pos * share_rows_q, share_rows_q, 0)
    share_o = lax.dynamic_slice_in_dim(total_o, worker_pos * share_rows_o, share_rows_o, 0)
    pseudo_q = share_q / workers
    pseudo_o = share_o / workers
    q_momentum_new = outer_mu * q_momentum + pseudo_q
    o_momentum_new = outer_mu * o_momentum + pseudo_o
    q_direction = pseudo_q + outer_mu * q_momentum_new
    o_direction = pseudo_o + outer_mu * o_momentum_new
    return (
        q_first_new[None],
        o_first_new[None],
        q_direction,
        o_direction,
        q_momentum_new,
        o_momentum_new,
    )


def solution(mesh):
    in_specs = (
        P(("worker", "fsdp"), None),
        P(("worker", "fsdp"), None),
        P(("worker", "fsdp"), None),
        P(("worker", "fsdp"), None),
        P(("worker", "fsdp")),
        P("worker", "fsdp", None),
        P("worker", "fsdp", None),
        P("worker", "fsdp", None),
        P("worker", "fsdp", None),
        P("worker", "fsdp", None),
        P("worker", "fsdp", None),
        P(("fsdp", "worker"), None),
        P(("fsdp", "worker"), None),
    )
    out_specs = (
        P("worker", "fsdp", None),
        P("worker", "fsdp", None),
        P(("fsdp", "worker"), None),
        P(("fsdp", "worker"), None),
        P(("fsdp", "worker"), None),
        P(("fsdp", "worker"), None),
    )
    return jax.shard_map(
        per_device, mesh=mesh, in_specs=in_specs, out_specs=out_specs, check_vma=False
    )
```

profile of v0, /device:TPU:0, one launch (start us, length us, event | category | flops | bytes accessed | tf_op | source)
XLA Modules:
  0.0 372.3 jit_solution(17039477943532699633)
XLA Ops:
  7.2 0.7 compare_convert_fusion
  8.0 1.9 broadcast_multiply_fusion.1
  9.9 0.0 all-gather.5.cloned.1.call-start
  10.0 2.5 broadcast_multiply_fusion
  12.5 1.3 copy.50
  13.8 7.0 %all-to-all-start = ((bf16[128,8,512]{0,2,1:T(8,128)(2,1)}), bf16[128,8,512]{0,2,1:T(8,128)(2,1)S(1)}, u32[]{:S(2)}, u32[]{:S(2)}) async-start(bf16[128,8,512]{0,2,1:T(8,128)(2,1)} %bitcast.1), calls=%async_computation | async-start | bytes 2097152 | tf_op jit(solution)/shard_map/all_to_all | solution.py:55
  20.8 1.0 copy.60
  21.8 3.4 copy.59
  25.3 5.6 %copy.72 = f32[1,256,4096]{1,2,0:T(8,128)} copy(f32[1,256,4096]{2,1,0:T(8,128)} %param.21) | data formatting | bytes 8388608 | tf_op args[8]
  30.9 4.1 %copy.73 = bf16[1,256,4096]{1,2,0:T(8,128)(2,1)} copy(bf16[1,256,4096]{2,1,0:T(8,128)(2,1)} %param.23) | data formatting | bytes 4194304 | tf_op args[10]
  35.0 3.9 %copy.49 = bf16[1,512,2048]{1,2,0:T(8,128)(2,1)} copy(bf16[1,512,2048]{2,1,0:T(8,128)(2,1)} %param.19) | data formatting | bytes 4194304 | tf_op args[6]
  38.9 5.4 %copy.69 = f32[1,512,2048]{1,2,0:T(8,128)} copy(f32[1,512,2048]{2,1,0:T(8,128)} %param.18) | data formatting | bytes 8388608 | tf_op args[5]
  44.3 3.9 %copy.70 = bf16[1,512,2048]{1,2,0:T(8,128)(2,1)} copy(bf16[1,512,2048]{2,1,0:T(8,128)(2,1)} %param.20) | data formatting | bytes 4194304 | tf_op args[7]
  48.2 7.1 %all-to-all-start.1 = ((bf16[128,8,256]{0,2,1:T(8,128)(2,1)}), bf16[128,8,256]{0,2,1:T(8,128)(2,1)}, u32[]{:S(2)}, u32[]{:S(2)}) async-start(bf16[128,8,256]{0,2,1:T(8,128)(2,1)} %bitcast.148), calls=%async_computation.1 | async-start | bytes 1048576 | tf_op jit(solution)/shard_map/all_to_all | solution.py:56
  55.4 40.4 %all-gather.3.cloned.1.call-done = bf16[1024,2048]{1,0:T(8,128)(2,1)} async-done(((bf16[128,2048]{1,0:T(8,128)(2,1)}), bf16[1024,2048]{1,0:T(8,128)(2,1)}) %all-gather.3.cloned.1.call-update) | async-done | bytes 4194320 | tf_op jit(solution)/shard_map/all_gather | solution.py:59
  95.8 1.9 fusion.24
  97.7 1.8 fusion.25
  99.5 0.7 fusion.26
  100.2 0.7 fusion.27
  101.0 0.7 fusion.28
  101.8 0.7 fusion.29
  102.5 2.0 fusion.30
  104.5 3.1 fusion.31
  107.6 8.5 %fusion.23 = (bf16[512,2048]{0,1:T(8,128)(2,1)}, f32[512,2048]{0,1:T(8,128)}) fusion(bf16[1,512,2048]{1,2,0:T(8,128)(2,1)S(1)} %copy-done.6, bf16[1,512,2048]{1,2,0:T(8,128)(2,1)S(1)} %copy-done, f32[1,512,2048]{1,2,0:T(8,128)S(1)} %copy-done.2, bf16[512,2048]{0,1:T(8,128)(2,1)} %fusion.31, bf16[512,2048]{0,1:T(8,128)(2,1)S(1)} %fusion.30, ...), kind=kLoop, calls=%fused_computation.37 | loop fusion | flops 30408704 | bytes 31457280 | tf_op jit(solution)/shard_map/convert_element_type | solution.py:75
  116.1 87.0 %all-gather.5.cloned.1.call-done = bf16[1024,4096]{1,0:T(8,128)(2,1)} async-done(((bf16[128,4096]{1,0:T(8,128)(2,1)}), bf16[1024,4096]{1,0:T(8,128)(2,1)}) %all-gather.5.cloned.1.call-update) | async-done | bytes 8388624 | tf_op jit(solution)/shard_map/all_gather | solution.py:60
  203.0 2.1 fusion
  205.2 2.5 fusion.1
  207.6 2.0 fusion.2
  209.6 1.6 fusion.3
  211.2 1.6 fusion.4
  212.8 1.7 fusion.5
  214.6 1.7 fusion.6
  216.3 1.6 fusion.7
  217.9 6.9 %fusion.22 = (bf16[256,4096]{0,1:T(8,128)(2,1)}, f32[256,4096]{0,1:T(8,128)}) fusion(bf16[1,256,4096]{1,2,0:T(8,128)(2,1)S(1)} %copy-done.5, bf16[1,256,4096]{1,2,0:T(8,128)(2,1)S(1)} %copy.59, f32[1,256,4096]{1,2,0:T(8,128)S(1)} %copy-done.1, bf16[256,4096]{0,1:T(8,128)(2,1)S(1)} %fusion.7, bf16[256,4096]{0,1:T(8,128)(2,1)S(1)} %fusion.6, ...), kind=kLoop, calls=%fused_computation.36 | loop fusion | flops 30408704 | bytes 31457280 | tf_op jit(solution)/shard_map/convert_element_type | solution.py:76
  224.8 0.9 copy-done.12
  225.8 2.0 copy.75
  227.7 0.3 copy.71
  228.1 5.0 %fusion.32 = bf16[1,512,2048]{1,2,0:T(8,128)(2,1)} fusion(f32[512,2048]{0,1:T(8,128)} %get-tuple-element.33, bf16[1,512,2048]{1,2,0:T(8,128)(2,1)} %copy.49), kind=kLoop, calls=%fused_computation.54 | loop fusion | flops 5242880 | bytes 8388608 | tf_op jit(solution)/shard_map/broadcast_in_dim | solution.py:90
  233.0 3.9 %copy.76 = bf16[1,512,2048]{2,1,0:T(8,128)(2,1)} copy(bf16[1,512,2048]{1,2,0:T(8,128)(2,1)} %fusion.32) | data formatting | bytes 4194304
  236.9 4.2 %fusion.33 = bf16[1,256,4096]{1,2,0:T(8,128)(2,1)} fusion(f32[256,4096]{0,1:T(8,128)} %get-tuple-element.31, bf16[1,256,4096]{1,2,0:T(8,128)(2,1)S(1)} %copy.59), kind=kLoop, calls=%fused_computation.55 | loop fusion | flops 5242880 | bytes 8388608 | tf_op jit(solution)/shard_map/broadcast_in_dim | solution.py:91
  241.2 4.2 %copy.77 = bf16[1,256,4096]{2,1,0:T(8,128)(2,1)} copy(bf16[1,256,4096]{1,2,0:T(8,128)(2,1)} %fusion.33) | data formatting | bytes 4194304
  245.4 107.6 %all-reduce.3.cloned.1.call-done = (bf16[512,2048]{0,1:T(8,128)(2,1)}, bf16[256,4096]{0,1:T(8,128)(2,1)}) async-done(((bf16[512,2048]{0,1:T(8,128)(2,1)}, bf16[256,4096]{0,1:T(8,128)(2,1)}), (bf16[512,2048]{0,1:T(8,128)(2,1)}, bf16[256,4096]{0,1:T(8,128)(2,1)})) %all-reduce.3.cloned.1.call-update) | async-done | bytes 4194320 | tf_op jit(solution)/shard_map/psum | solution.py:75
  353.0 3.7 %multiply_add_fusion = (f32[16,4096]{0,1:T(8,128)}, f32[16,4096]{0,1:T(8,128)}) fusion(bf16[256,4096]{0,1:T(8,128)(2,1)} %get-tuple-element.25, s32[]{:T(128)S(6)} %select_n.7, f32[16,4096]{0,1:T(8,128)S(1)} %copy-done.4), kind=kLoop, calls=%fused_computation.56 | loop fusion | flops 327680 | bytes 917508 | tf_op jit(solution)/shard_map/add | solution.py:88
  356.7 2.9 copy.79
  359.5 2.9 copy.81
  362.4 1.3 multiply_add_fusion.1
  363.8 1.0 copy.78
  364.8 1.0 copy.80
  (33 shorter events, 0.2 us)
Async XLA Ops:
  7.2 5.3 %copy-start.9 = (bf16[128,4096]{1,0:T(8,128)(2,1)S(1)}, bf16[128,4096]{1,0:T(8,128)(2,1)}, u32[]{:S(2)}) copy-start(bf16[128,4096]{1,0:T(8,128)(2,1)} %param.13) | copy-start | bytes 3145732
  7.2 88.6 %all-gather.3.cloned.1.call-start = ((), (), s32[]{:S(2)}) async-start(), calls=%async_computation.2 | async-start | bytes 4718592 | tf_op jit(solution)/shard_map/all_gather | solution.py:59
  9.9 10.9 %copy-start.10 = (bf16[128,2048]{1,0:T(8,128)(2,1)S(1)}, bf16[128,2048]{1,0:T(8,128)(2,1)}, u32[]{:S(2)}) copy-start(bf16[128,2048]{1,0:T(8,128)(2,1)} %param.14) | copy-start | bytes 1572868
  9.9 193.1 %all-gather.5.cloned.1.call-start = ((), (), s32[]{:S(2)}) async-start(), calls=%async_computation.3 | async-start | bytes 9437184 | tf_op jit(solution)/shard_map/all_gather | solution.py:60
  13.8 34.4 %all-to-all-start = ((bf16[128,8,512]{0,2,1:T(8,128)(2,1)}), bf16[128,8,512]{0,2,1:T(8,128)(2,1)S(1)}, u32[]{:S(2)}, u32[]{:S(2)}) async-start(bf16[128,8,512]{0,2,1:T(8,128)(2,1)} %bitcast.1), calls=%async_computation | async-start | bytes 2097152 | tf_op jit(solution)/shard_map/all_to_all | solution.py:55
  48.2 53.5 %copy-start.8 = (bf16[128,8,512]{0,2,1:T(8,128)(2,1)}, bf16[128,8,512]{0,2,1:T(8,128)(2,1)S(1)}, u32[]{:S(2)}) copy-start(bf16[128,8,512]{0,2,1:T(8,128)(2,1)S(1)} %all-to-all-done) | copy-start | bytes 3145732
  48.2 67.8 %all-to-all-start.1 = ((bf16[128,8,256]{0,2,1:T(8,128)(2,1)}), bf16[128,8,256]{0,2,1:T(8,128)(2,1)}, u32[]{:S(2)}, u32[]{:S(2)}) async-start(bf16[128,8,256]{0,2,1:T(8,128)(2,1)} %bitcast.148), calls=%async_computation.1 | async-start | bytes 1048576 | tf_op jit(solution)/shard_map/all_to_all | solution.py:56
  55.3 297.6 %all-reduce.3.cloned.1.call-start = ((), (), s32[]{:S(2)}) async-start(), calls=%async_computation.4 | async-start | bytes 8388608 | tf_op jit(solution)/shard_map/psum | solution.py:75
  95.8 3.7 copy-start.7
  101.0 6.6 %copy-start.6 = (bf16[1,512,2048]{1,2,0:T(8,128)(2,1)S(1)}, bf16[1,512,2048]{1,2,0:T(8,128)(2,1)}, u32[]{:S(2)}) copy-start(bf16[1,512,2048]{1,2,0:T(8,128)(2,1)} %copy.70) | copy-start | bytes 6291460
  101.7 5.8 %copy-start = (bf16[1,512,2048]{1,2,0:T(8,128)(2,1)S(1)}, bf16[1,512,2048]{1,2,0:T(8,128)(2,1)}, u32[]{:S(2)}) copy-start(bf16[1,512,2048]{1,2,0:T(8,128)(2,1)} %copy.49) | copy-start | bytes 6291460
  101.7 5.8 %copy-start.2 = (f32[1,512,2048]{1,2,0:T(8,128)S(1)}, f32[1,512,2048]{1,2,0:T(8,128)}, u32[]{:S(2)}) copy-start(f32[1,512,2048]{1,2,0:T(8,128)} %copy.69) | copy-start | bytes 12582916
  203.0 6.6 %copy-start.3 = (bf16[1024,4096]{1,0:T(8,128)(2,1)S(1)}, bf16[1024,4096]{1,0:T(8,128)(2,1)}, u32[]{:S(2)}) copy-start(bf16[1024,4096]{1,0:T(8,128)(2,1)} %all-gather.5.cloned.1.call-done) | copy-start | bytes 25165828
  212.8 5.1 %copy-start.1 = (f32[1,256,4096]{1,2,0:T(8,128)S(1)}, f32[1,256,4096]{1,2,0:T(8,128)}, u32[]{:S(2)}) copy-start(f32[1,256,4096]{1,2,0:T(8,128)} %copy.72) | copy-start | bytes 12582916
  212.8 5.1 %copy-start.5 = (bf16[1,256,4096]{1,2,0:T(8,128)(2,1)S(1)}, bf16[1,256,4096]{1,2,0:T(8,128)(2,1)}, u32[]{:S(2)}) copy-start(bf16[1,256,4096]{1,2,0:T(8,128)(2,1)} %copy.73) | copy-start | bytes 6291460
  224.8 0.9 copy-start.12
  224.8 2.9 copy-start.11
  241.2 111.8 %copy-start.4 = (f32[16,4096]{0,1:T(8,128)S(1)}, f32[16,4096]{0,1:T(8,128)}, u32[]{:S(2)}) copy-start(f32[16,4096]{0,1:T(8,128)} %copy.75) | copy-start | bytes 786436
Sparse Core Ops, SparseCore 0:
  10.4 85.3 all-gather.2
  98.1 104.8 all-gather.4
  224.9 127.9 all-reduce.2
where the time goes:
time: 374 us; the launch traced here: 372 us
  waiting for transfers between devices  235 us (63%)
  local copies, waits for them, and re-layouts  47.9 us (13%)
  other arithmetic  34.8 us (9%)
  matrix products  26.5 us (7%)
  starting transfers between devices  14.2 us (4%)
  between operations  14 us (4%)
    psum x1, waiting for transfers between devices, per_device(): lax.psum(moved_q.astype(jnp.bfloat16), 'worker').astype(jnp.float32)  108 us
    all_gather x1, waiting for transfers between devices, per_device(): piece_o = lax.all_gather(o_cot, 'fsdp', axis=0, tiled=True)  87 us
    unnamed x41, local copies, waits for them, and re-layouts  45.9 us
    all_gather x1, waiting for transfers between devices, per_device(): piece_q = lax.all_gather(q_cot, 'fsdp', axis=0, tiled=True)  40.4 us
    dot_general x16, matrix products, cross_rows(): lax.dot_general(left, right, (((0,), (0,)), ((), ())), preferred_element_...  26.5 us
    convert_element_type x1, other arithmetic, per_device(): moved_q.astype(jnp.bfloat16)  8.47 us
  transfers between devices with their start and end apart: 5, of which 3 were waited for; matrix products, arithmetic and copies ran while one was open for 19% of the time, Pallas kernels for 0%

commit v1 on v0

--- a/solution.py
+++ b/solution.py
@@ -72,7 +72,7 @@
     o_first_new, moved_o = adam_moved(grads_o, o_offset[0], o_first[0], o_second[0])
     workers = lax.axis_size("worker")
     total_q, total_o = (
-        lax.psum(moved_q.astype(jnp.bfloat16), "worker").astype(jnp.float32),
+        jnp.sum(lax.all_gather(moved_q.astype(jnp.bfloat16), "worker"), axis=0).astype(jnp.float32),
         lax.psum(moved_o.astype(jnp.bfloat16), "worker").astype(jnp.float32),
     )
     worker_pos = lax.axis_index("worker")

time: 374 us -> 580 us (1.55)
  waiting for transfers between devices: 235 us -> 384 us
  other arithmetic: 34.8 us -> 57.5 us
  local copies, waits for them, and re-layouts: 47.9 us -> 67.7 us
  matrix products: 26.5 us -> 39.8 us
    all_gather x0 -> x1, waiting for transfers between devices: none -> 164 us  [per_device(): lax.all_gather(moved_q.astype(jnp.bfloat16), 'worker')]
    psum x1, waiting for transfers between devices: 108 us -> 86.1 us  [per_device(): lax.psum(moved_o.astype(jnp.bfloat16), 'worker').astype(jnp.float32)]
    unnamed x41 -> x38, local copies, waits for them, and re-layouts: 45.9 us -> 65.8 us
    reduce_sum x0 -> x1, other arithmetic: none -> 17.2 us  [per_device(): jnp.sum(lax.all_gather(moved_q.astype(jnp.bfloat16), 'worker'), axis=0)]
    dot_general x16, matrix products: 26.5 us -> 39.8 us  [cross_rows(): lax.dot_general(left, right, (((0,), (0,)), ((), ())), preferred_element_...]
  transfers between devices with their start and end apart: 5 -> 6, of which waited for: 3 -> 4; matrix products, arithmetic and copies ran while one was open for 19% -> 15% of each run, Pallas kernels for 0% -> 0%
where the time goes in v1:
time: 580 us; the launch traced here: 577 us
  waiting for transfers between devices  384 us (66%)
  local copies, waits for them, and re-layouts  67.7 us (12%)
  other arithmetic  57.5 us (10%)
  matrix products  39.8 us (7%)
  starting transfers between devices  14.7 us (3%)
  between operations  13.9 us (2%)
    all_gather x1, waiting for transfers between devices, per_device(): lax.all_gather(moved_q.astype(jnp.bfloat16), 'worker')  164 us
    all_gather x1, waiting for transfers between devices, per_device(): piece_o = lax.all_gather(o_cot, 'fsdp', axis=0, tiled=True)  92.7 us
    psum x1, waiting for transfers between devices, per_device(): lax.psum(moved_o.astype(jnp.bfloat16), 'worker').astype(jnp.float32)  86.1 us
    unnamed x38, local copies, waits for them, and re-layouts  65.8 us
    all_gather x1, waiting for transfers between devices, per_device(): piece_q = lax.all_gather(q_cot, 'fsdp', axis=0, tiled=True)  41.3 us
    dot_general x16, matrix products, cross_rows(): lax.dot_general(left, right, (((0,), (0,)), ((), ())), preferred_element_...  39.8 us
    reduce_sum x1, other arithmetic, per_device(): jnp.sum(lax.all_gather(moved_q.astype(jnp.bfloat16), 'worker'), axis=0)  17.2 us
  transfers between devices with their start and end apart: 6, of which 4 were waited for; matrix products, arithmetic and copies ran while one was open for 15% of the time, Pallas kernels for 0%

profile of v1, /device:TPU:0, one launch (start us, length us, event | category | flops | bytes accessed | tf_op | source)
XLA Modules:
  0.0 577.3 jit_solution(3760308833074584585)
XLA Ops:
  8.0 2.0 broadcast_multiply_fusion.1
  10.0 2.5 broadcast_multiply_fusion
  12.5 1.3 copy.74
  13.8 7.0 %all-to-all-start = ((bf16[128,8,512]{0,2,1:T(8,128)(2,1)}), bf16[128,8,512]{0,2,1:T(8,128)(2,1)S(1)}, u32[]{:S(2)}, u32[]{:S(2)}) async-start(bf16[128,8,512]{0,2,1:T(8,128)(2,1)} %bitcast.1), calls=%async_computation | async-start | bytes 2097152 | tf_op jit(solution)/shard_map/all_to_all | solution.py:55
  20.9 2.5 copy.94
  23.4 4.0 copy.73
  27.3 5.5 copy.93
  32.9 2.4 copy.97
  35.3 3.3 copy.83
  38.6 5.7 copy.96
  44.3 2.1 copy.84
  46.3 7.2 %all-to-all-start.1 = ((bf16[128,8,256]{0,2,1:T(8,128)(2,1)}), bf16[128,8,256]{0,2,1:T(8,128)(2,1)}, u32[]{:S(2)}, u32[]{:S(2)}) async-start(bf16[128,8,256]{0,2,1:T(8,128)(2,1)} %bitcast.154), calls=%async_computation.1 | async-start | bytes 1048576 | tf_op jit(solution)/shard_map/all_to_all | solution.py:56
  53.7 41.3 %all-gather.5.cloned.1.call-done = bf16[1024,2048]{1,0:T(8,128)(2,1)} async-done(((bf16[128,2048]{1,0:T(8,128)(2,1)}), bf16[1024,2048]{1,0:T(8,128)(2,1)}) %all-gather.5.cloned.1.call-update) | async-done | bytes 4194320 | tf_op jit(solution)/shard_map/all_gather | solution.py:59
  95.0 3.3 fusion.31
  98.3 3.1 fusion.30
  101.4 2.0 fusion.29
  103.5 2.1 fusion.28
  105.5 2.1 fusion.27
  107.7 2.1 fusion.26
  109.8 92.7 %all-gather.7.cloned.1.call-done = bf16[1024,4096]{1,0:T(8,128)(2,1)} async-done(((bf16[128,4096]{1,0:T(8,128)(2,1)}), bf16[1024,4096]{1,0:T(8,128)(2,1)}) %all-gather.7.cloned.1.call-update) | async-done | bytes 8388624 | tf_op jit(solution)/shard_map/all_gather | solution.py:60
  202.5 2.1 fusion.7
  204.6 2.5 fusion.6
  207.1 2.0 fusion.5
  209.1 2.9 fusion.4
  212.0 2.9 fusion.3
  215.0 3.0 fusion.2
  218.0 2.9 fusion.1
  220.9 2.9 fusion
  223.8 9.3 %fusion.22 = (bf16[256,4096]{0,1:T(8,128)(2,1)}, f32[256,4096]{0,1:T(8,128)}) fusion(bf16[1,256,4096]{1,2,0:T(8,128)(2,1)S(1)} %copy-done.5, bf16[1,256,4096]{1,2,0:T(8,128)(2,1)S(1)} %copy.83, f32[1,256,4096]{1,2,0:T(8,128)S(1)} %copy-done.1, bf16[256,4096]{0,1:T(8,128)(2,1)S(1)} %fusion.7, bf16[256,4096]{0,1:T(8,128)(2,1)S(1)} %fusion.6, ...), kind=kLoop, calls=%fused_computation.37 | loop fusion | flops 30408704 | bytes 31457280 | tf_op jit(solution)/shard_map/convert_element_type | solution.py:76
  233.5 1.9 fusion.25
  235.4 1.8 fusion.24
  237.2 10.4 %fusion.23 = (bf16[512,2048]{0,1:T(8,128)(2,1)}, f32[512,2048]{0,1:T(8,128)}) fusion(bf16[1,512,2048]{1,2,0:T(8,128)(2,1)S(1)} %copy-done.4, bf16[1,512,2048]{1,2,0:T(8,128)(2,1)S(1)} %copy-done, f32[1,512,2048]{1,2,0:T(8,128)} %copy.93, bf16[512,2048]{0,1:T(8,128)(2,1)} %fusion.31, bf16[512,2048]{0,1:T(8,128)(2,1)} %fusion.30, ...), kind=kLoop, calls=%fused_computation.38 | loop fusion | flops 30408704 | bytes 31457280 | tf_op jit(solution)/shard_map/convert_element_type | solution.py:75
  248.0 1.0 broadcast_multiply_fusion.2
  249.0 1.9 copy.99
  251.0 5.0 fusion.32
  256.0 3.9 copy.100
  259.9 4.2 fusion.33
  264.1 4.2 copy.101
  268.3 86.1 %all-reduce.2.cloned.1.call-done = bf16[256,4096]{0,1:T(8,128)(2,1)} async-done(((bf16[256,4096]{0,1:T(8,128)(2,1)}), bf16[256,4096]{0,1:T(8,128)(2,1)}) %all-reduce.2.cloned.1.call-update) | async-done | bytes 2097168 | tf_op jit(solution)/shard_map/psum | solution.py:76
  354.4 3.8 multiply_add_fusion
  358.2 2.9 copy.103
  361.0 2.9 copy.105
  363.9 163.5 %all-gather.9.cloned.1.call-done = bf16[8192,2048]{0,1:T(8,128)(2,1)} async-done(((bf16[512,2048]{0,1:T(8,128)(2,1)}), bf16[8192,2048]{0,1:T(8,128)(2,1)}) %all-gather.9.cloned.1.call-update) | async-done | bytes 33554448 | tf_op jit(solution)/shard_map/all_gather | solution.py:75
  527.5 22.7 %copy.106 = bf16[256,8,16,512]{3,2,1,0:T(8,128)(2,1)} copy(bf16[256,8,16,512]{3,1,2,0:T(8,128)(2,1)} %bitcast.145) | data formatting | bytes 67108864
  550.2 17.2 %bitcast_reduce_fusion = bf16[512,2048]{0,1:T(8,128)(2,1)} fusion(bf16[256,8,16,512]{3,2,1,0:T(8,128)(2,1)} %copy.106), kind=kLoop, calls=%fused_computation | loop fusion | flops 15728640 | bytes 35651584 | tf_op jit(solution)/shard_map/reduce_sum | solution.py:75
  567.4 1.3 multiply_add_fusion.1
  568.7 1.0 copy.102
  569.7 1.0 copy.104
  (34 shorter events, 1.7 us)
Async XLA Ops:
  7.2 5.3 copy-start.9
  7.2 87.8 %all-gather.5.cloned.1.call-start = ((), (), s32[]{:S(2)}) async-start(), calls=%async_computation.2 | async-start | bytes 4718592 | tf_op jit(solution)/shard_map/all_gather | solution.py:59
  9.9 10.9 %copy-start.7 = (bf16[1,512,2048]{2,1,0:T(8,128)(2,1)S(1)}, bf16[1,512,2048]{2,1,0:T(8,128)(2,1)}, u32[]{:S(2)}) copy-start(bf16[1,512,2048]{2,1,0:T(8,128)(2,1)} %param.20) | copy-start | bytes 6291460
  9.9 192.6 %all-gather.7.cloned.1.call-start = ((), (), s32[]{:S(2)}) async-start(), calls=%async_computation.3 | async-start | bytes 9437184 | tf_op jit(solution)/shard_map/all_gather | solution.py:60
  13.8 32.5 %all-to-all-start = ((bf16[128,8,512]{0,2,1:T(8,128)(2,1)}), bf16[128,8,512]{0,2,1:T(8,128)(2,1)S(1)}, u32[]{:S(2)}, u32[]{:S(2)}) async-start(bf16[128,8,512]{0,2,1:T(8,128)(2,1)} %bitcast.1), calls=%async_computation | async-start | bytes 2097152 | tf_op jit(solution)/shard_map/all_to_all | solution.py:55
  27.3 5.5 copy-start.8
  46.3 63.5 %all-to-all-start.1 = ((bf16[128,8,256]{0,2,1:T(8,128)(2,1)}), bf16[128,8,256]{0,2,1:T(8,128)(2,1)}, u32[]{:S(2)}, u32[]{:S(2)}) async-start(bf16[128,8,256]{0,2,1:T(8,128)(2,1)} %bitcast.154), calls=%async_computation.1 | async-start | bytes 1048576 | tf_op jit(solution)/shard_map/all_to_all | solution.py:56
  53.5 300.9 %all-reduce.2.cloned.1.call-start = ((), (), s32[]{:S(2)}) async-start(), calls=%async_computation.4 | async-start | bytes 4194304 | tf_op jit(solution)/shard_map/psum | solution.py:76
  95.0 6.4 %copy-start.6 = (bf16[1024,2048]{1,0:T(8,128)(2,1)S(1)}, bf16[1024,2048]{1,0:T(8,128)(2,1)}, u32[]{:S(2)}) copy-start(bf16[1024,2048]{1,0:T(8,128)(2,1)} %all-gather.5.cloned.1.call-done) | copy-start | bytes 12582916
  202.5 6.6 %copy-start.2 = (bf16[1024,4096]{1,0:T(8,128)(2,1)S(1)}, bf16[1024,4096]{1,0:T(8,128)(2,1)}, u32[]{:S(2)}) copy-start(bf16[1024,4096]{1,0:T(8,128)(2,1)} %all-gather.7.cloned.1.call-done) | copy-start | bytes 25165828
  215.0 8.9 %copy-start.1 = (f32[1,256,4096]{1,2,0:T(8,128)S(1)}, f32[1,256,4096]{1,2,0:T(8,128)}, u32[]{:S(2)}) copy-start(f32[1,256,4096]{1,2,0:T(8,128)} %copy.96) | copy-start | bytes 12582916
  215.0 8.9 %copy-start.5 = (bf16[1,256,4096]{1,2,0:T(8,128)(2,1)S(1)}, bf16[1,256,4096]{1,2,0:T(8,128)(2,1)}, u32[]{:S(2)}) copy-start(bf16[1,256,4096]{1,2,0:T(8,128)(2,1)} %copy.97) | copy-start | bytes 6291460
  233.2 294.3 %all-gather.9.cloned.1.call-start = ((), (), s32[]{:S(2)}) async-start(), calls=%async_computation.5 | async-start | bytes 35651584 | tf_op jit(solution)/shard_map/all_gather | solution.py:75
  233.5 3.7 copy-start
  233.5 3.7 copy-start.4
  237.2 10.5 %copy-start.10 = (f32[32,2048]{1,0:T(8,128)S(1)}, f32[32,2048]{1,0:T(8,128)}, u32[]{:S(2)}) copy-start(f32[32,2048]{1,0:T(8,128)} %param.24) | copy-start | bytes 786436
  264.1 90.3 %copy-start.3 = (f32[16,4096]{0,1:T(8,128)S(1)}, f32[16,4096]{0,1:T(8,128)}, u32[]{:S(2)}) copy-start(f32[16,4096]{0,1:T(8,128)} %copy.99) | copy-start | bytes 786436
Sparse Core Ops, SparseCore 0:
  10.4 84.5 all-gather.4
  97.4 105.1 all-gather.6
  233.3 121.0 all-reduce.1
  355.9 171.4 all-gather.8
